TPU v7x, 32 devices: a whole 2x2x4 slice. The times are simulated.
32 devices in a mesh: scen: 2 (over y), blk: 16 (over z, x, core).
Axes of the slice: x: 2, y: 2, z: 4, core: 2. Of those that a mesh axis runs over, the one named last changes fastest.
Arguments:
- returns: bfloat16 [128, 8192], P(('scen', 'blk')), may hold values from -6 to 6
- vol_hist: float32 [128, 8192], P(('scen', 'blk')), may hold values from 0.5 to 5.5, as said below
- vol_now: float32 [8192], replicated, may hold values from 0.5 to 2
- sensitivity: bfloat16 [4096, 128, 128], P('blk'), may hold values from -0.109375 to 0.109375
- block_pairs: int32 [4096, 3], P('blk'), may hold values from 0 to 63, as said below
- book_order: int32 [32], replicated, may hold values from 0 to 31, each once
Outputs:
- profit_loss: float32 [128, 4096], P('scen', 'blk')
- book_rms: float32 [4096], P('blk')
Inputs may be any that keep to these rules, and one draw needn't show every extreme that they name: `block_pairs`: each index k of blk holds 256 slots; their factor blocks lie in k * 4 to k * 4 + 3; on each index the live slots come first; some index has all 256 slots live. `vol_hist`: positive volatilities.
All inputs are finite; a program needn't handle non-finite values.
Results may differ from a plain program's by a relative error of at most 0.0029.
Values may be sent and summed in bfloat16 or wider, within the bound.
No kernel may reach another device: no remote copies, remote signals or barrier semaphores. Data moves between devices by JAX's collectives and lax.ppermute only.
A program may use at most 64 MiB of HBM per device.

v0:
```python
import functools

import jax
import jax.numpy as jnp
from jax import lax
from jax.experimental import pallas as pl
from jax.experimental.pallas import tpu as pltpu
from jax.sharding import PartitionSpec as P

UNROLL = 32
VMEM_LIMIT = 32 * 1024 * 1024
VMEM = pl.BlockSpec(memory_space=pltpu.VMEM)
HBM = pl.BlockSpec(memory_space=pltpu.HBM)


def accumulate(
    groups, shocks, pairs_hbm, order_hbm, sens_hbm, kept, sent, acc, sens, pairs, order, position, small, arrived
):
    slots = sens.shape[0]
    factors, _, block = shocks.shape
    chunks = arrived.shape[0]
    chunk = slots // chunks
    half = kept.shape[0]
    books = 2 * half
    per_owner = books // groups
    index = lax.axis_index("blk")
    core = index & 1

    def fetch(c):
        span = pl.ds(c * chunk, chunk)
        return pltpu.make_async_copy(sens_hbm.at[span], sens.at[span], arrived.at[c])

    get_order = pltpu.make_async_copy(order_hbm, order, small.at[0])
    get_pairs = pltpu.make_async_copy(pairs_hbm, pairs, small.at[1])
    get_order.start()
    get_pairs.start()
    for c in range(chunks):
        fetch(c).start()
    acc[...] = jnp.zeros_like(acc)
    get_order.wait()
    for p in range(books):
        owner = p // per_owner
        place = (owner // 2) * per_owner + p % per_owner
        position[order[p]] = place + half * ((owner & 1) ^ core)
    position[books] = books
    get_pairs.wait()
    first_factor = index * factors

    def work(c, carry):
        fetch(c).wait()

        @pl.when(pairs[2, c * chunk] != 0)
        def _():
            for u in range(chunk):
                k = c * chunk + u
                book = jnp.where(pairs[2, k] != 0, pairs[1, k], books)
                f = pairs[0, k] - first_factor
                acc[position[book]] += jnp.dot(shocks[f], sens[k], preferred_element_type=jnp.float32)

        return carry

    lax.fori_loop(0, chunks, work, 0)
    kept[...] = acc[:half]
    sent[...] = acc[half:books].astype(sent.dtype)


def shards(returns, vol_hist, vol_now, sensitivity, block_pairs, book_order):
    groups = lax.axis_size("blk")
    own_rows, width = returns.shape
    slots, block, _ = sensitivity.shape
    own = width // groups
    rows = groups * own_rows
    books = book_order.shape[0]
    siblings = [(i, i ^ 1) for i in range(groups)]
    rescaled = (returns.astype(jnp.float32) * vol_now[None, :] / vol_hist).astype(jnp.bfloat16)
    outgoing = rescaled.reshape(own_rows, groups, own).swapaxes(0, 1)
    incoming = lax.all_to_all(outgoing, "blk", 0, 0)
    shocks = incoming.reshape(rows, own // block, block).transpose(1, 0, 2)
    chunks = slots // UNROLL
    kept, sent = pl.pallas_call(
        functools.partial(accumulate, groups),
        in_specs=[VMEM, HBM, HBM, HBM],
        out_specs=[VMEM, VMEM],
        out_shape=[
            jax.ShapeDtypeStruct((books // 2, rows, block), jnp.float32),
            jax.ShapeDtypeStruct((books // 2, rows, block), jnp.bfloat16),
        ],
        scratch_shapes=[
            pltpu.VMEM((books + 1, rows, block), jnp.float32),
            pltpu.VMEM(sensitivity.shape, sensitivity.dtype),
            pltpu.SMEM((3, slots), jnp.int32),
            pltpu.SMEM((books,), jnp.int32),
            pltpu.SMEM((books + 1,), jnp.int32),
            pltpu.SemaphoreType.DMA((2,)),
            pltpu.SemaphoreType.DMA((chunks,)),
        ],
        compiler_params=pltpu.CompilerParams(vmem_limit_bytes=VMEM_LIMIT),
        cost_estimate=pl.CostEstimate(
            flops=2 * slots * rows * block * block,
            bytes_accessed=2 * slots * block * block,
            transcendentals=0,
        ),
    )(shocks, *(pltpu.with_memory_space_constraint(x, pltpu.HBM) for x in (block_pairs.T, book_order, sensitivity)))
    across = lax.ppermute(sent, "blk", siblings)
    per_owner = books // groups
    chips = groups // 2
    chip_sum = (kept + across.astype(jnp.float32)).astype(jnp.bfloat16).reshape(chips, per_owner, rows, block)
    same_core = [list(range(c, groups, 2)) for c in range(2)]
    arrived = lax.all_to_all(chip_sum, "blk", 0, 0, axis_index_groups=same_core)
    owned = jnp.sum(arrived.astype(jnp.float32), axis=0)
    profit_loss = owned.transpose(1, 0, 2).reshape(rows, per_owner * block)
    spans = lax.axis_size("scen")
    squares = jnp.sum(owned * owned, axis=1).reshape(-1)
    if spans == 2:
        squares = squares + lax.ppermute(squares, "scen", [(0, 1), (1, 0)])
    else:
        squares = lax.psum(squares, "scen")
    book_rms = jnp.sqrt(squares / (rows * spans) + 1e-06)
    return (profit_loss, book_rms)


def solution(mesh):
    return jax.shard_map(
        shards,
        mesh=mesh,
        in_specs=(
            P(("scen", "blk"), None),
            P(("scen", "blk"), None),
            P(),
            P("blk", None, None),
            P("blk", None),
            P(),
        ),
        out_specs=(P("scen", "blk"), P("blk")),
        check_vma=False,
    )
```

profile of v0, /device:TPU:0, one launch (start us, length us, event | category | flops | bytes accessed | tf_op | source)
XLA Modules:
  0.0 37.4 jit_solution(15006681383518575268)
XLA Ops:
  0.6 1.0 %fusion = bf16[4,8192]{1,0:T(4,128)(2,1)S(1)} fusion(f32[4,8192]{1,0:T(4,128)} %param.7, bf16[4,8192]{1,0:T(4,128)(2,1)} %param.6, f32[8192]{0:T(1024)} %param.8), kind=kLoop, calls=%fused_computation.3 | loop fusion | flops 131072 | bytes 294912 | tf_op jit(solution)/shard_map/convert_element_type | solution.py:75
  1.6 14.1 %all_to_all.10 = bf16[16,4,512]{2,1,0:T(4,128)(2,1)S(1)} all-to-all(bf16[16,4,512]{2,1,0:T(4,128)(2,1)S(1)} %bitcast.18), channel_id=1, replica_groups=mesh['scen'=2,'blk'=16] {'blk'}, dimensions={0} | all-to-all | bytes 131072 | tf_op jit(solution)/shard_map/all_to_all | solution.py:77
  15.7 3.6 %shard_map.77 = (f32[16,64,128]{2,1,0:T(8,128)S(1)}, bf16[16,64,128]{2,1,0:T(8,128)(2,1)S(1)}) custom-call(bf16[4,64,128]{2,1,0:T(8,128)(2,1)S(1)} %bitcast.16, s32[3,256]{1,0:T(4,128)} %bitcast.19, s32[32]{0:T(128)} %order_hbm.1, bf16[256,128,128]{2,1,0:T(8,128)(2,1)} %sens_hbm.1), custom_call_target="tpu_custom_call" | custom-call | flops 536870912 | bytes 8388608 | tf_op jit(solution)/shard_map/pallas_call | solution.py:80
  19.3 0.1 collective-permute-start
  19.4 1.5 %collective-permute-done = bf16[16,64,128]{2,1,0:T(8,128)(2,1)S(1)} collective-permute-done((bf16[16,64,128]{2,1,0:T(8,128)(2,1)S(1)}, bf16[16,64,128]{2,1,0:T(8,128)(2,1)S(1)}, u32[]{:S(2)}, u32[]{:S(2)}) %collective-permute-start) | collective-permute-done | bytes 262176 | tf_op jit(solution)/shard_map/ppermute | solution.py:104
  20.9 0.1 add_convert_fusion
  21.0 12.1 %all_to_all.11 = bf16[8,2,64,128]{3,2,1,0:T(8,128)(2,1)S(1)} all-to-all(bf16[8,2,64,128]{3,2,1,0:T(8,128)(2,1)S(1)} %bitcast.17), channel_id=1, replica_groups={{0,2,4,6,8,10,12,14},{1,3,5,7,9,11,13,15},{16,18,20,22,24,26,28,30},{17..., dimensions={0} | all-to-all | bytes 524288 | tf_op jit(solution)/shard_map/all_to_all | solution.py:109
  33.2 1.6 %collective-permute-start.1 = (f32[256]{0:T(256)S(1)}, f32[256]{0:T(256)S(1)}, u32[]{:S(2)}, u32[]{:S(2)}) collective-permute-start(f32[256]{0:T(256)S(1)} %bitcast.20), channel_id=1, source_target_pairs={{0,16},{16,0},{1,17},{17,1},{2,18},{18,2},{3,19},{19,3},{4,20},{20... | collective-permute-start | bytes 3080 | tf_op jit(solution)/shard_map/ppermute | solution.py:115
  34.8 0.6 %copy_bitcast_fusion = f32[64,256]{1,0:T(8,128)} fusion(f32[2,64,128]{2,1,0:T(8,128)S(1)} %convert_reduce_fusion), kind=kLoop, calls=%fused_computation.4 | loop fusion | bytes 131072 | tf_op jit(solution)/shard_map/reshape | solution.py:111
  35.4 1.4 %collective-permute-done.1 = f32[256]{0:T(256)S(1)} collective-permute-done((f32[256]{0:T(256)S(1)}, f32[256]{0:T(256)S(1)}, u32[]{:S(2)}, u32[]{:S(2)}) %collective-permute-start.1) | collective-permute-done | bytes 1056 | tf_op jit(solution)/shard_map/ppermute | solution.py:115
  36.8 0.6 %add_sqrt_fusion = f32[256]{0:T(256)} fusion(f32[256]{0:T(256)S(1)} %collective-permute-done.1, f32[2,128]{1,0:T(2,128)S(1)} %multiply_reduce_fusion), kind=kLoop, calls=%fused_computation.7 | loop fusion | flops 768 | bytes 3072 | tf_op jit(solution)/shard_map/sqrt | solution.py:118
  (4 shorter events, 0.1 us)
Async XLA Ops:
  19.3 1.6 %collective-permute-start = (bf16[16,64,128]{2,1,0:T(8,128)(2,1)S(1)}, bf16[16,64,128]{2,1,0:T(8,128)(2,1)S(1)}, u32[]{:S(2)}, u32[]{:S(2)}) collective-permute-start(bf16[16,64,128]{2,1,0:T(8,128)(2,1)S(1)} %get-tuple-element.5), channel_id=1, source_target_pairs={{0,1},{1,0},{2,3},{3,2},{4,5},{5,4},{6,7},{7,6},{8,9},{9,8},{10,11... | collective-permute-start | bytes 786440 | tf_op jit(solution)/shard_map/ppermute | solution.py:104
  33.2 3.6 %collective-permute-start.1 = (f32[256]{0:T(256)S(1)}, f32[256]{0:T(256)S(1)}, u32[]{:S(2)}, u32[]{:S(2)}) collective-permute-start(f32[256]{0:T(256)S(1)} %bitcast.20), channel_id=1, source_target_pairs={{0,16},{16,0},{1,17},{17,1},{2,18},{18,2},{3,19},{19,3},{4,20},{20... | collective-permute-start | bytes 3080 | tf_op jit(solution)/shard_map/ppermute | solution.py:115
where the time goes:
time: 37.5 us; the launch traced here: 37.4 us
  blocking collectives  26.2 us (70%)
  Pallas kernels  3.56 us (9%)
  waiting for transfers between devices  2.94 us (8%)
  other arithmetic  1.71 us (5%)
  starting transfers between devices  1.65 us (4%)
  local copies, waits for them, and re-layouts  0.68 us (2%)
  between operations  0.68 us (2%)
    all_to_all x1, blocking collectives, shards(): incoming = lax.all_to_all(outgoing, 'blk', 0, 0)  14.1 us
    all_to_all x1, blocking collectives, shards(): arrived = lax.all_to_all(chip_sum, 'blk', 0, 0, axis_index_groups=same_core)  12.1 us
    pallas_call x1, Pallas kernels, shards(): pl.pallas_call(functools.partial(accumulate, groups), in_specs=[VMEM, HBM...  3.56 us
    ppermute x1, starting transfers between devices, shards(): squares = squares + lax.ppermute(squares, 'scen', [(0, 1), (1, 0)])  1.58 us
    ppermute x1, waiting for transfers between devices, shards(): across = lax.ppermute(sent, 'blk', siblings)  1.52 us
    ppermute x1, waiting for transfers between devices, shards(): squares = squares + lax.ppermute(squares, 'scen', [(0, 1), (1, 0)])  1.42 us
    convert_element_type x1, other arithmetic, shards(): (returns.astype(jnp.float32) * vol_now[None, :] / vol_hist).astype(jnp.bf...  1 us
  transfers between devices with their start and end apart: 2, of which 2 were waited for; matrix products, arithmetic and copies ran while one was open for 2% of the time, Pallas kernels for 0%

commit v1 on v0

--- a/solution.py
+++ b/solution.py
@@ -7,7 +7,8 @@
 from jax.experimental.pallas import tpu as pltpu
 from jax.sharding import PartitionSpec as P
 
-UNROLL = 32
+CHUNK = 16
+UNROLL = 64
 VMEM_LIMIT = 32 * 1024 * 1024
 VMEM = pl.BlockSpec(memory_space=pltpu.VMEM)
 HBM = pl.BlockSpec(memory_space=pltpu.HBM)
@@ -46,20 +47,25 @@
     get_pairs.wait()
     first_factor = index * factors
 
-    def work(c, carry):
-        fetch(c).wait()
-
-        @pl.when(pairs[2, c * chunk] != 0)
+    def work(g, carry):
+        @pl.when(pairs[2, g * UNROLL] != 0)
         def _():
-            for u in range(chunk):
-                k = c * chunk + u
+            for u in range(UNROLL):
+                if u % chunk == 0:
+                    fetch(g * (UNROLL // chunk) + u // chunk).wait()
+                k = g * UNROLL + u
                 book = jnp.where(pairs[2, k] != 0, pairs[1, k], books)
                 f = pairs[0, k] - first_factor
                 acc[position[book]] += jnp.dot(shocks[f], sens[k], preferred_element_type=jnp.float32)
 
+        @pl.when(pairs[2, g * UNROLL] == 0)
+        def _():
+            for c in range(UNROLL // chunk):
+                fetch(g * (UNROLL // chunk) + c).wait()
+
         return carry
 
-    lax.fori_loop(0, chunks, work, 0)
+    lax.fori_loop(0, slots // UNROLL, work, 0)
     kept[...] = acc[:half]
     sent[...] = acc[half:books].astype(sent.dtype)
 
@@ -76,7 +82,7 @@
     outgoing = rescaled.reshape(own_rows, groups, own).swapaxes(0, 1)
     incoming = lax.all_to_all(outgoing, "blk", 0, 0)
     shocks = incoming.reshape(rows, own // block, block).transpose(1, 0, 2)
-    chunks = slots // UNROLL
+    chunks = slots // CHUNK
     kept, sent = pl.pallas_call(
         functools.partial(accumulate, groups),
         in_specs=[VMEM, HBM, HBM, HBM],

time: 37.5 us -> 38.1 us (1.016)
  blocking collectives: 26.2 us -> 26.6 us
    all_to_all x1, blocking collectives: 12.1 us -> 12.6 us  [shards(): arrived = lax.all_to_all(chip_sum, 'blk', 0, 0, axis_index_groups=same_core)]
where the time goes in v1:
time: 38.1 us; the launch traced here: 37.9 us
  blocking collectives  26.6 us (70%)
  Pallas kernels  3.6 us (9%)
  waiting for transfers between devices  2.94 us (8%)
  other arithmetic  1.71 us (4%)
  starting transfers between devices  1.65 us (4%)
  local copies, waits for them, and re-layouts  0.68 us (2%)
  between operations  0.68 us (2%)
    all_to_all x1, blocking collectives, shards(): incoming = lax.all_to_all(outgoing, 'blk', 0, 0)  14.1 us
    all_to_all x1, blocking collectives, shards(): arrived = lax.all_to_all(chip_sum, 'blk', 0, 0, axis_index_groups=same_core)  12.6 us
    pallas_call x1, Pallas kernels, shards(): pl.pallas_call(functools.partial(accumulate, groups), in_specs=[VMEM, HBM...  3.6 us
    ppermute x1, starting transfers between devices, shards(): squares = squares + lax.ppermute(squares, 'scen', [(0, 1), (1, 0)])  1.58 us
    ppermute x1, waiting for transfers between devices, shards(): across = lax.ppermute(sent, 'blk', siblings)  1.52 us
    ppermute x1, waiting for transfers between devices, shards(): squares = squares + lax.ppermute(squares, 'scen', [(0, 1), (1, 0)])  1.42 us
    convert_element_type x1, other arithmetic, shards(): (returns.astype(jnp.float32) * vol_now[None, :] / vol_hist).astype(jnp.bf...  1 us
  transfers between devices with their start and end apart: 2, of which 2 were waited for; matrix products, arithmetic and copies ran while one was open for 2% of the time, Pallas kernels for 0%

profile of v1, /device:TPU:0, one launch (start us, length us, event | category | flops | bytes accessed | tf_op | source)
XLA Modules:
  0.0 37.9 jit_solution(9191178501750130985)
XLA Ops:
  0.6 1.0 %fusion = bf16[4,8192]{1,0:T(4,128)(2,1)S(1)} fusion(f32[4,8192]{1,0:T(4,128)} %param.7, bf16[4,8192]{1,0:T(4,128)(2,1)} %param.6, f32[8192]{0:T(1024)} %param.8), kind=kLoop, calls=%fused_computation.3 | loop fusion | flops 131072 | bytes 294912 | tf_op jit(solution)/shard_map/convert_element_type | solution.py:81
  1.6 14.1 %all_to_all.10 = bf16[16,4,512]{2,1,0:T(4,128)(2,1)S(1)} all-to-all(bf16[16,4,512]{2,1,0:T(4,128)(2,1)S(1)} %bitcast.18), channel_id=1, replica_groups=mesh['scen'=2,'blk'=16] {'blk'}, dimensions={0} | all-to-all | bytes 131072 | tf_op jit(solution)/shard_map/all_to_all | solution.py:83
  15.7 3.6 %shard_map.77 = (f32[16,64,128]{2,1,0:T(8,128)S(1)}, bf16[16,64,128]{2,1,0:T(8,128)(2,1)S(1)}) custom-call(bf16[4,64,128]{2,1,0:T(8,128)(2,1)S(1)} %bitcast.16, s32[3,256]{1,0:T(4,128)} %bitcast.19, s32[32]{0:T(128)} %order_hbm.1, bf16[256,128,128]{2,1,0:T(8,128)(2,1)} %sens_hbm.1), custom_call_target="tpu_custom_call" | custom-call | flops 536870912 | bytes 8388608 | tf_op jit(solution)/shard_map/pallas_call | solution.py:86
  19.3 0.1 collective-permute-start
  19.4 1.5 %collective-permute-done = bf16[16,64,128]{2,1,0:T(8,128)(2,1)S(1)} collective-permute-done((bf16[16,64,128]{2,1,0:T(8,128)(2,1)S(1)}, bf16[16,64,128]{2,1,0:T(8,128)(2,1)S(1)}, u32[]{:S(2)}, u32[]{:S(2)}) %collective-permute-start) | collective-permute-done | bytes 262176 | tf_op jit(solution)/shard_map/ppermute | solution.py:110
  20.9 0.1 add_convert_fusion
  21.0 12.6 %all_to_all.11 = bf16[8,2,64,128]{3,2,1,0:T(8,128)(2,1)S(1)} all-to-all(bf16[8,2,64,128]{3,2,1,0:T(8,128)(2,1)S(1)} %bitcast.17), channel_id=1, replica_groups={{0,2,4,6,8,10,12,14},{1,3,5,7,9,11,13,15},{16,18,20,22,24,26,28,30},{17..., dimensions={0} | all-to-all | bytes 524288 | tf_op jit(solution)/shard_map/all_to_all | solution.py:115
  33.7 1.6 %collective-permute-start.1 = (f32[256]{0:T(256)S(1)}, f32[256]{0:T(256)S(1)}, u32[]{:S(2)}, u32[]{:S(2)}) collective-permute-start(f32[256]{0:T(256)S(1)} %bitcast.20), channel_id=1, source_target_pairs={{0,16},{16,0},{1,17},{17,1},{2,18},{18,2},{3,19},{19,3},{4,20},{20... | collective-permute-start | bytes 3080 | tf_op jit(solution)/shard_map/ppermute | solution.py:121
  35.2 0.6 %copy_bitcast_fusion = f32[64,256]{1,0:T(8,128)} fusion(f32[2,64,128]{2,1,0:T(8,128)S(1)} %convert_reduce_fusion), kind=kLoop, calls=%fused_computation.4 | loop fusion | bytes 131072 | tf_op jit(solution)/shard_map/reshape | solution.py:117
  35.9 1.4 %collective-permute-done.1 = f32[256]{0:T(256)S(1)} collective-permute-done((f32[256]{0:T(256)S(1)}, f32[256]{0:T(256)S(1)}, u32[]{:S(2)}, u32[]{:S(2)}) %collective-permute-start.1) | collective-permute-done | bytes 1056 | tf_op jit(solution)/shard_map/ppermute | solution.py:121
  37.3 0.6 %add_sqrt_fusion = f32[256]{0:T(256)} fusion(f32[256]{0:T(256)S(1)} %collective-permute-done.1, f32[2,128]{1,0:T(2,128)S(1)} %multiply_reduce_fusion), kind=kLoop, calls=%fused_computation.7 | loop fusion | flops 768 | bytes 3072 | tf_op jit(solution)/shard_map/sqrt | solution.py:124
  (4 shorter events, 0.1 us)
Async XLA Ops:
  19.3 1.6 %collective-permute-start = (bf16[16,64,128]{2,1,0:T(8,128)(2,1)S(1)}, bf16[16,64,128]{2,1,0:T(8,128)(2,1)S(1)}, u32[]{:S(2)}, u32[]{:S(2)}) collective-permute-start(bf16[16,64,128]{2,1,0:T(8,128)(2,1)S(1)} %get-tuple-element.5), channel_id=1, source_target_pairs={{0,1},{1,0},{2,3},{3,2},{4,5},{5,4},{6,7},{7,6},{8,9},{9,8},{10,11... | collective-permute-start | bytes 786440 | tf_op jit(solution)/shard_map/ppermute | solution.py:110
  33.7 3.6 %collective-permute-start.1 = (f32[256]{0:T(256)S(1)}, f32[256]{0:T(256)S(1)}, u32[]{:S(2)}, u32[]{:S(2)}) collective-permute-start(f32[256]{0:T(256)S(1)} %bitcast.20), channel_id=1, source_target_pairs={{0,16},{16,0},{1,17},{17,1},{2,18},{18,2},{3,19},{19,3},{4,20},{20... | collective-permute-start | bytes 3080 | tf_op jit(solution)/shard_map/ppermute | solution.py:121

commit v2 on v0

--- a/solution.py
+++ b/solution.py
@@ -17,7 +17,7 @@
     groups, shocks, pairs_hbm, order_hbm, sens_hbm, kept, sent, acc, sens, pairs, order, position, small, arrived
 ):
     slots = sens.shape[0]
-    factors, _, block = shocks.shape
+    factors = shocks.shape[0]
     chunks = arrived.shape[0]
     chunk = slots // chunks
     half = kept.shape[0]
@@ -31,7 +31,7 @@
         return pltpu.make_async_copy(sens_hbm.at[span], sens.at[span], arrived.at[c])
 
     get_order = pltpu.make_async_copy(order_hbm, order, small.at[0])
-    get_pairs = pltpu.make_async_copy(pairs_hbm, pairs, small.at[1])
+    get_pairs = pltpu.make_async_copy(pairs_hbm, pairs.at[:, pl.ds(0, slots)], small.at[1])
     get_order.start()
     get_pairs.start()
     for c in range(chunks):
@@ -43,23 +43,76 @@
         place = (owner // 2) * per_owner + p % per_owner
         position[order[p]] = place + half * ((owner & 1) ^ core)
     position[books] = books
+    first_factor = index * factors
     get_pairs.wait()
-    first_factor = index * factors
+    for u in range(chunk):
+        pairs[0, slots + u] = first_factor
+        pairs[1, slots + u] = 0
+        pairs[2, slots + u] = 0
+    padding = chunks
+    quads = chunk // 4
+    rows, block = shocks.shape[1:]
+    none = jnp.zeros((rows, block), shocks.dtype)
 
-    def work(c, carry):
+    def count(c, busy):
+        return busy + jnp.where(pairs[2, c * chunk] != 0, 1, 0)
+
+    busy = lax.fori_loop(0, chunks, count, 0)
+
+    def on_units(*units):
+        def push(q, rhs):
+            pltpu.matmul_push_rhs(rhs, (q // 2) % 2, q % 2)
+
+        def stage(c, q):
+            k = c * chunk + 4 * q
+            upper = jnp.concatenate([sens[k], sens[k + 1]], axis=1)
+            lower = jnp.concatenate([sens[k + 2], sens[k + 3]], axis=1)
+            push(q, jnp.concatenate([upper, lower], axis=0))
+
+        def multiply(c, q):
+            for t in range(4):
+                scenarios = shocks[pairs[0, c * chunk + 4 * q + t] - first_factor]
+                halves = [scenarios, none] if t < 2 else [none, scenarios]
+                staged = (q // 2) % 2 if t == 0 else None
+                pltpu.matmul_acc_lhs(units[4 * q + t], jnp.concatenate(halves, axis=1), load_staged_rhs=staged)
+
+        def collect(c, q):
+            for t in range(4):
+                k = c * chunk + 4 * q + t
+                book = jnp.where(pairs[2, k] != 0, pairs[1, k], books)
+                side = (t % 2) * block
+                acc[position[book]] += pltpu.matmul_pop(units[4 * q + t])[:, side : side + block]
+
+        zeros = jnp.zeros((2 * block, 2 * block), sens.dtype)
+        for q in range(quads - 4, quads):
+            push(q, zeros)
+            if q < quads - 2:
+                multiply(padding, q)
+
+        def work(c, carry):
+            fetch(c).wait()
+            before = jnp.where(c == 0, padding, c - 1)
+            for q in range(quads):
+                stage(c, q)
+                multiply(*((before, q - 2 + quads) if q < 2 else (c, q - 2)))
+                collect(*((before, q - 4 + quads) if q < 4 else (c, q - 4)))
+            return carry
+
+        lax.fori_loop(0, busy, work, 0)
+        last = jnp.where(busy == 0, padding, busy - 1)
+        for q in range(quads - 4, quads):
+            if q >= quads - 2:
+                multiply(last, q)
+        for q in range(quads - 4, quads):
+            collect(last, q)
+
+    pl.run_scoped(on_units, *[pltpu.ACC(k // 4 % 2)((rows, 2 * block), jnp.float32) for k in range(chunk)])
+
+    def drop(c, carry):
         fetch(c).wait()
-
-        @pl.when(pairs[2, c * chunk] != 0)
-        def _():
-            for u in range(chunk):
-                k = c * chunk + u
-                book = jnp.where(pairs[2, k] != 0, pairs[1, k], books)
-                f = pairs[0, k] - first_factor
-                acc[position[book]] += jnp.dot(shocks[f], sens[k], preferred_element_type=jnp.float32)
-
         return carry
 
-    lax.fori_loop(0, chunks, work, 0)
+    lax.fori_loop(busy, chunks, drop, 0)
     kept[...] = acc[:half]
     sent[...] = acc[half:books].astype(sent.dtype)
 
@@ -88,7 +141,7 @@
         scratch_shapes=[
             pltpu.VMEM((books + 1, rows, block), jnp.float32),
             pltpu.VMEM(sensitivity.shape, sensitivity.dtype),
-            pltpu.SMEM((3, slots), jnp.int32),
+            pltpu.SMEM((3, slots + UNROLL), jnp.int32),
             pltpu.SMEM((books,), jnp.int32),
             pltpu.SMEM((books + 1,), jnp.int32),
             pltpu.SemaphoreType.DMA((2,)),
@@ -120,7 +173,11 @@
 
 
 def solution(mesh):
-    return jax.shard_map(
+    def on_mesh(*args):
+        with jax.sharding.use_abstract_mesh(mesh.abstract_mesh):
+            return whole(*args)
+
+    whole = jax.shard_map(
         shards,
         mesh=mesh,
         in_specs=(
@@ -134,3 +191,4 @@
         out_specs=(P("scen", "blk"), P("blk")),
         check_vma=False,
     )
+    return on_mesh

time: 37.5 us -> 37.4 us (level)
  no operation moved by 1% of the time
where the time goes in v2:
time: 37.4 us; the launch traced here: 37.2 us
  blocking collectives  26 us (70%)
  Pallas kernels  3.56 us (10%)
  waiting for transfers between devices  2.94 us (8%)
  other arithmetic  1.71 us (5%)
  starting transfers between devices  1.66 us (4%)
  local copies, waits for them, and re-layouts  0.68 us (2%)
  between operations  0.68 us (2%)
    all_to_all x1, blocking collectives, shards(): incoming = lax.all_to_all(outgoing, 'blk', 0, 0)  14.1 us
    all_to_all x1, blocking collectives, shards(): arrived = lax.all_to_all(chip_sum, 'blk', 0, 0, axis_index_groups=same_core)  11.9 us
    pallas_call x1, Pallas kernels, shards(): pl.pallas_call(functools.partial(accumulate, groups), in_specs=[VMEM, HBM...  3.56 us
    ppermute x1, starting transfers between devices, shards(): squares = squares + lax.ppermute(squares, 'scen', [(0, 1), (1, 0)])  1.58 us
    ppermute x1, waiting for transfers between devices, shards(): across = lax.ppermute(sent, 'blk', siblings)  1.52 us
    ppermute x1, waiting for transfers between devices, shards(): squares = squares + lax.ppermute(squares, 'scen', [(0, 1), (1, 0)])  1.41 us
    convert_element_type x1, other arithmetic, shards(): (returns.astype(jnp.float32) * vol_now[None, :] / vol_hist).astype(jnp.bf...  1 us
  transfers between devices with their start and end apart: 2, of which 2 were waited for; matrix products, arithmetic and copies ran while one was open for 2% of the time, Pallas kernels for 0%

profile of v2, /device:TPU:0, one launch (start us, length us, event | category | flops | bytes accessed | tf_op | source)
XLA Modules:
  0.0 37.2 jit_solution(2972144133711436949)
XLA Ops:
  0.6 1.0 %fusion = bf16[4,8192]{1,0:T(4,128)(2,1)S(1)} fusion(f32[4,8192]{1,0:T(4,128)} %param.7, bf16[4,8192]{1,0:T(4,128)(2,1)} %param.6, f32[8192]{0:T(1024)} %param.8), kind=kLoop, calls=%fused_computation.3 | loop fusion | flops 131072 | bytes 294912 | tf_op jit(solution)/shard_map/convert_element_type | solution.py:128
  1.6 14.1 %all_to_all.10 = bf16[16,4,512]{2,1,0:T(4,128)(2,1)S(1)} all-to-all(bf16[16,4,512]{2,1,0:T(4,128)(2,1)S(1)} %bitcast.18), channel_id=1, replica_groups=mesh['scen'=2,'blk'=16] {'blk'}, dimensions={0} | all-to-all | bytes 131072 | tf_op jit(solution)/shard_map/all_to_all | solution.py:130
  15.7 3.6 %shard_map.77 = (f32[16,64,128]{2,1,0:T(8,128)S(1)}, bf16[16,64,128]{2,1,0:T(8,128)(2,1)S(1)}) custom-call(bf16[4,64,128]{2,1,0:T(8,128)(2,1)S(1)} %bitcast.16, s32[3,256]{1,0:T(4,128)} %bitcast.19, s32[32]{0:T(128)} %order_hbm.1, bf16[256,128,128]{2,1,0:T(8,128)(2,1)} %sens_hbm.1), custom_call_target="tpu_custom_call" | custom-call | flops 536870912 | bytes 8388608 | tf_op jit(solution)/shard_map/pallas_call | solution.py:133
  19.3 0.1 collective-permute-start
  19.4 1.5 %collective-permute-done = bf16[16,64,128]{2,1,0:T(8,128)(2,1)S(1)} collective-permute-done((bf16[16,64,128]{2,1,0:T(8,128)(2,1)S(1)}, bf16[16,64,128]{2,1,0:T(8,128)(2,1)S(1)}, u32[]{:S(2)}, u32[]{:S(2)}) %collective-permute-start) | collective-permute-done | bytes 262176 | tf_op jit(solution)/shard_map/ppermute | solution.py:157
  20.9 0.1 add_convert_fusion
  21.0 11.9 %all_to_all.11 = bf16[8,2,64,128]{3,2,1,0:T(8,128)(2,1)S(1)} all-to-all(bf16[8,2,64,128]{3,2,1,0:T(8,128)(2,1)S(1)} %bitcast.17), channel_id=1, replica_groups={{0,2,4,6,8,10,12,14},{1,3,5,7,9,11,13,15},{16,18,20,22,24,26,28,30},{17..., dimensions={0} | all-to-all | bytes 524288 | tf_op jit(solution)/shard_map/all_to_all | solution.py:162
  33.0 1.6 %collective-permute-start.1 = (f32[256]{0:T(256)S(1)}, f32[256]{0:T(256)S(1)}, u32[]{:S(2)}, u32[]{:S(2)}) collective-permute-start(f32[256]{0:T(256)S(1)} %bitcast.20), channel_id=1, source_target_pairs={{0,16},{16,0},{1,17},{17,1},{2,18},{18,2},{3,19},{19,3},{4,20},{20... | collective-permute-start | bytes 3080 | tf_op jit(solution)/shard_map/ppermute | solution.py:168
  34.6 0.6 %copy_bitcast_fusion = f32[64,256]{1,0:T(8,128)} fusion(f32[2,64,128]{2,1,0:T(8,128)S(1)} %convert_reduce_fusion), kind=kLoop, calls=%fused_computation.4 | loop fusion | bytes 131072 | tf_op jit(solution)/shard_map/reshape | solution.py:164
  35.2 1.4 %collective-permute-done.1 = f32[256]{0:T(256)S(1)} collective-permute-done((f32[256]{0:T(256)S(1)}, f32[256]{0:T(256)S(1)}, u32[]{:S(2)}, u32[]{:S(2)}) %collective-permute-start.1) | collective-permute-done | bytes 1056 | tf_op jit(solution)/shard_map/ppermute | solution.py:168
  36.6 0.6 %add_sqrt_fusion = f32[256]{0:T(256)} fusion(f32[256]{0:T(256)S(1)} %collective-permute-done.1, f32[2,128]{1,0:T(2,128)S(1)} %multiply_reduce_fusion), kind=kLoop, calls=%fused_computation.7 | loop fusion | flops 768 | bytes 3072 | tf_op jit(solution)/shard_map/sqrt | solution.py:171
  (4 shorter events, 0.1 us)
Async XLA Ops:
  19.3 1.6 %collective-permute-start = (bf16[16,64,128]{2,1,0:T(8,128)(2,1)S(1)}, bf16[16,64,128]{2,1,0:T(8,128)(2,1)S(1)}, u32[]{:S(2)}, u32[]{:S(2)}) collective-permute-start(bf16[16,64,128]{2,1,0:T(8,128)(2,1)S(1)} %get-tuple-element.5), channel_id=1, source_target_pairs={{0,1},{1,0},{2,3},{3,2},{4,5},{5,4},{6,7},{7,6},{8,9},{9,8},{10,11... | collective-permute-start | bytes 786440 | tf_op jit(solution)/shard_map/ppermute | solution.py:157
  33.0 3.6 %collective-permute-start.1 = (f32[256]{0:T(256)S(1)}, f32[256]{0:T(256)S(1)}, u32[]{:S(2)}, u32[]{:S(2)}) collective-permute-start(f32[256]{0:T(256)S(1)} %bitcast.20), channel_id=1, source_target_pairs={{0,16},{16,0},{1,17},{17,1},{2,18},{18,2},{3,19},{19,3},{4,20},{20... | collective-permute-start | bytes 3080 | tf_op jit(solution)/shard_map/ppermute | solution.py:168

commit v3 on v2

--- a/solution.py
+++ b/solution.py
@@ -8,6 +8,8 @@
 from jax.sharding import PartitionSpec as P
 
 UNROLL = 32
+SIZES = (4, 2, 2, 4, 2, 2)
+LAG = 6
 VMEM_LIMIT = 32 * 1024 * 1024
 VMEM = pl.BlockSpec(memory_space=pltpu.VMEM)
 HBM = pl.BlockSpec(memory_space=pltpu.HBM)
@@ -50,9 +52,16 @@
         pairs[1, slots + u] = 0
         pairs[2, slots + u] = 0
     padding = chunks
-    quads = chunk // 4
     rows, block = shocks.shape[1:]
     none = jnp.zeros((rows, block), shocks.dtype)
+    blank = jnp.zeros((block, block), sens.dtype)
+
+    packs = []
+    for j, size in enumerate(SIZES):
+        for unit in range(2):
+            first = unit * (chunk // 2) + sum(SIZES[:j])
+            packs.append((first, size, unit, j % 2))
+    many = len(packs)
 
     def count(c, busy):
         return busy + jnp.where(pairs[2, c * chunk] != 0, 1, 0)
@@ -60,53 +69,66 @@
     busy = lax.fori_loop(0, chunks, count, 0)
 
     def on_units(*units):
-        def push(q, rhs):
-            pltpu.matmul_push_rhs(rhs, (q // 2) % 2, q % 2)
-
-        def stage(c, q):
-            k = c * chunk + 4 * q
-            upper = jnp.concatenate([sens[k], sens[k + 1]], axis=1)
-            lower = jnp.concatenate([sens[k + 2], sens[k + 3]], axis=1)
-            push(q, jnp.concatenate([upper, lower], axis=0))
-
-        def multiply(c, q):
-            for t in range(4):
-                scenarios = shocks[pairs[0, c * chunk + 4 * q + t] - first_factor]
-                halves = [scenarios, none] if t < 2 else [none, scenarios]
-                staged = (q // 2) % 2 if t == 0 else None
-                pltpu.matmul_acc_lhs(units[4 * q + t], jnp.concatenate(halves, axis=1), load_staged_rhs=staged)
-
-        def collect(c, q):
-            for t in range(4):
-                k = c * chunk + 4 * q + t
+        def push(i, rhs):
+            _, _, unit, staged = packs[i]
+            pltpu.matmul_push_rhs(rhs, staged, unit)
+
+        def stage(c, i):
+            k = c * chunk + packs[i][0]
+            if packs[i][1] == 4:
+                tiles = [[sens[k], sens[k + 1]], [sens[k + 2], sens[k + 3]]]
+            else:
+                tiles = [[sens[k], blank], [blank, sens[k + 1]]]
+            push(i, jnp.concatenate([jnp.concatenate(row, axis=1) for row in tiles], axis=0))
+
+        def multiply(c, i):
+            first, size, _, staged = packs[i]
+            scenarios = [shocks[pairs[0, c * chunk + first + t] - first_factor] for t in range(size)]
+            if size == 4:
+                passes = [[x, none] if t < 2 else [none, x] for t, x in enumerate(scenarios)]
+            else:
+                passes = [scenarios]
+            for t, halves in enumerate(passes):
+                target = units[spot[i] + t]
+                pltpu.matmul_acc_lhs(target, jnp.concatenate(halves, axis=1), load_staged_rhs=None if t else staged)
+
+        def collect(c, i):
+            first, size, _, _ = packs[i]
+            popped = [pltpu.matmul_pop(units[spot[i] + t]) for t in range(4 if size == 4 else 1)]
+            for t in range(size):
+                k = c * chunk + first + t
                 book = jnp.where(pairs[2, k] != 0, pairs[1, k], books)
                 side = (t % 2) * block
-                acc[position[book]] += pltpu.matmul_pop(units[4 * q + t])[:, side : side + block]
+                acc[position[book]] += popped[t if size == 4 else 0][:, side : side + block]
 
         zeros = jnp.zeros((2 * block, 2 * block), sens.dtype)
-        for q in range(quads - 4, quads):
-            push(q, zeros)
-            if q < quads - 2:
-                multiply(padding, q)
+        for i in range(many - LAG, many):
+            push(i, zeros)
+            if i < many - 2:
+                multiply(padding, i)
 
         def work(c, carry):
             fetch(c).wait()
             before = jnp.where(c == 0, padding, c - 1)
-            for q in range(quads):
-                stage(c, q)
-                multiply(*((before, q - 2 + quads) if q < 2 else (c, q - 2)))
-                collect(*((before, q - 4 + quads) if q < 4 else (c, q - 4)))
+            for i in range(many):
+                stage(c, i)
+                multiply(*((before, i - 2 + many) if i < 2 else (c, i - 2)))
+                collect(*((before, i - LAG + many) if i < LAG else (c, i - LAG)))
             return carry
 
         lax.fori_loop(0, busy, work, 0)
         last = jnp.where(busy == 0, padding, busy - 1)
-        for q in range(quads - 4, quads):
-            if q >= quads - 2:
-                multiply(last, q)
-        for q in range(quads - 4, quads):
-            collect(last, q)
-
-    pl.run_scoped(on_units, *[pltpu.ACC(k // 4 % 2)((rows, 2 * block), jnp.float32) for k in range(chunk)])
+        for i in range(many - 2, many):
+            multiply(last, i)
+        for i in range(many - LAG, many):
+            collect(last, i)
+
+    spot = []
+    held = []
+    for _, size, unit, _ in packs:
+        spot.append(len(held))
+        held += [pltpu.ACC(unit)((rows, 2 * block), jnp.float32)] * (4 if size == 4 else 1)
+    pl.run_scoped(on_units, *held)
 
     def drop(c, carry):
         fetch(c).wait()

time: 37.4 us -> 37.4 us (level)
  no operation moved by 1% of the time
where the time goes in v3:
time: 37.4 us; the launch traced here: 37.2 us
  blocking collectives  26 us (70%)
  Pallas kernels  3.56 us (10%)
  waiting for transfers between devices  2.94 us (8%)
  other arithmetic  1.71 us (5%)
  starting transfers between devices  1.66 us (4%)
  local copies, waits for them, and re-layouts  0.68 us (2%)
  between operations  0.68 us (2%)
    all_to_all x1, blocking collectives, shards(): incoming = lax.all_to_all(outgoing, 'blk', 0, 0)  14.1 us
    all_to_all x1, blocking collectives, shards(): arrived = lax.all_to_all(chip_sum, 'blk', 0, 0, axis_index_groups=same_core)  11.9 us
    pallas_call x1, Pallas kernels, shards(): pl.pallas_call(functools.partial(accumulate, groups), in_specs=[VMEM, HBM...  3.56 us
    ppermute x1, starting transfers between devices, shards(): squares = squares + lax.ppermute(squares, 'scen', [(0, 1), (1, 0)])  1.58 us
    ppermute x1, waiting for transfers between devices, shards(): across = lax.ppermute(sent, 'blk', siblings)  1.52 us
    ppermute x1, waiting for transfers between devices, shards(): squares = squares + lax.ppermute(squares, 'scen', [(0, 1), (1, 0)])  1.41 us
    convert_element_type x1, other arithmetic, shards(): (returns.astype(jnp.float32) * vol_now[None, :] / vol_hist).astype(jnp.bf...  1 us
  transfers between devices with their start and end apart: 2, of which 2 were waited for; matrix products, arithmetic and copies ran while one was open for 2% of the time, Pallas kernels for 0%

profile of v3, /device:TPU:0, one launch (start us, length us, event | category | flops | bytes accessed | tf_op | source)
XLA Modules:
  0.0 37.2 jit_solution(18247245194199207785)
XLA Ops:
  0.6 1.0 %fusion = bf16[4,8192]{1,0:T(4,128)(2,1)S(1)} fusion(f32[4,8192]{1,0:T(4,128)} %param.7, bf16[4,8192]{1,0:T(4,128)(2,1)} %param.6, f32[8192]{0:T(1024)} %param.8), kind=kLoop, calls=%fused_computation.3 | loop fusion | flops 131072 | bytes 294912 | tf_op jit(solution)/shard_map/convert_element_type | solution.py:150
  1.6 14.1 %all_to_all.10 = bf16[16,4,512]{2,1,0:T(4,128)(2,1)S(1)} all-to-all(bf16[16,4,512]{2,1,0:T(4,128)(2,1)S(1)} %bitcast.18), channel_id=1, replica_groups=mesh['scen'=2,'blk'=16] {'blk'}, dimensions={0} | all-to-all | bytes 131072 | tf_op jit(solution)/shard_map/all_to_all | solution.py:152
  15.7 3.6 %shard_map.77 = (f32[16,64,128]{2,1,0:T(8,128)S(1)}, bf16[16,64,128]{2,1,0:T(8,128)(2,1)S(1)}) custom-call(bf16[4,64,128]{2,1,0:T(8,128)(2,1)S(1)} %bitcast.16, s32[3,256]{1,0:T(4,128)} %bitcast.19, s32[32]{0:T(128)} %order_hbm.1, bf16[256,128,128]{2,1,0:T(8,128)(2,1)} %sens_hbm.1), custom_call_target="tpu_custom_call" | custom-call | flops 536870912 | bytes 8388608 | tf_op jit(solution)/shard_map/pallas_call | solution.py:155
  19.3 0.1 collective-permute-start
  19.4 1.5 %collective-permute-done = bf16[16,64,128]{2,1,0:T(8,128)(2,1)S(1)} collective-permute-done((bf16[16,64,128]{2,1,0:T(8,128)(2,1)S(1)}, bf16[16,64,128]{2,1,0:T(8,128)(2,1)S(1)}, u32[]{:S(2)}, u32[]{:S(2)}) %collective-permute-start) | collective-permute-done | bytes 262176 | tf_op jit(solution)/shard_map/ppermute | solution.py:179
  20.9 0.1 add_convert_fusion
  21.0 11.9 %all_to_all.11 = bf16[8,2,64,128]{3,2,1,0:T(8,128)(2,1)S(1)} all-to-all(bf16[8,2,64,128]{3,2,1,0:T(8,128)(2,1)S(1)} %bitcast.17), channel_id=1, replica_groups={{0,2,4,6,8,10,12,14},{1,3,5,7,9,11,13,15},{16,18,20,22,24,26,28,30},{17..., dimensions={0} | all-to-all | bytes 524288 | tf_op jit(solution)/shard_map/all_to_all | solution.py:184
  33.0 1.6 %collective-permute-start.1 = (f32[256]{0:T(256)S(1)}, f32[256]{0:T(256)S(1)}, u32[]{:S(2)}, u32[]{:S(2)}) collective-permute-start(f32[256]{0:T(256)S(1)} %bitcast.20), channel_id=1, source_target_pairs={{0,16},{16,0},{1,17},{17,1},{2,18},{18,2},{3,19},{19,3},{4,20},{20... | collective-permute-start | bytes 3080 | tf_op jit(solution)/shard_map/ppermute | solution.py:190
  34.6 0.6 %copy_bitcast_fusion = f32[64,256]{1,0:T(8,128)} fusion(f32[2,64,128]{2,1,0:T(8,128)S(1)} %convert_reduce_fusion), kind=kLoop, calls=%fused_computation.4 | loop fusion | bytes 131072 | tf_op jit(solution)/shard_map/reshape | solution.py:186
  35.2 1.4 %collective-permute-done.1 = f32[256]{0:T(256)S(1)} collective-permute-done((f32[256]{0:T(256)S(1)}, f32[256]{0:T(256)S(1)}, u32[]{:S(2)}, u32[]{:S(2)}) %collective-permute-start.1) | collective-permute-done | bytes 1056 | tf_op jit(solution)/shard_map/ppermute | solution.py:190
  36.6 0.6 %add_sqrt_fusion = f32[256]{0:T(256)} fusion(f32[256]{0:T(256)S(1)} %collective-permute-done.1, f32[2,128]{1,0:T(2,128)S(1)} %multiply_reduce_fusion), kind=kLoop, calls=%fused_computation.7 | loop fusion | flops 768 | bytes 3072 | tf_op jit(solution)/shard_map/sqrt | solution.py:193
  (4 shorter events, 0.1 us)
Async XLA Ops:
  19.3 1.6 %collective-permute-start = (bf16[16,64,128]{2,1,0:T(8,128)(2,1)S(1)}, bf16[16,64,128]{2,1,0:T(8,128)(2,1)S(1)}, u32[]{:S(2)}, u32[]{:S(2)}) collective-permute-start(bf16[16,64,128]{2,1,0:T(8,128)(2,1)S(1)} %get-tuple-element.5), channel_id=1, source_target_pairs={{0,1},{1,0},{2,3},{3,2},{4,5},{5,4},{6,7},{7,6},{8,9},{9,8},{10,11... | collective-permute-start | bytes 786440 | tf_op jit(solution)/shard_map/ppermute | solution.py:179
  33.0 3.6 %collective-permute-start.1 = (f32[256]{0:T(256)S(1)}, f32[256]{0:T(256)S(1)}, u32[]{:S(2)}, u32[]{:S(2)}) collective-permute-start(f32[256]{0:T(256)S(1)} %bitcast.20), channel_id=1, source_target_pairs={{0,16},{16,0},{1,17},{17,1},{2,18},{18,2},{3,19},{19,3},{4,20},{20... | collective-permute-start | bytes 3080 | tf_op jit(solution)/shard_map/ppermute | solution.py:190

commit v4 on v3

--- a/solution.py
+++ b/solution.py
@@ -39,14 +39,8 @@
     for c in range(chunks):
         fetch(c).start()
     acc[...] = jnp.zeros_like(acc)
-    get_order.wait()
-    for p in range(books):
-        owner = p // per_owner
-        place = (owner // 2) * per_owner + p % per_owner
-        position[order[p]] = place + half * ((owner & 1) ^ core)
     position[books] = books
     first_factor = index * factors
-    get_pairs.wait()
     for u in range(chunk):
         pairs[0, slots + u] = first_factor
         pairs[1, slots + u] = 0
@@ -62,11 +56,6 @@
             first = unit * (chunk // 2) + sum(SIZES[:j])
             packs.append((first, size, unit, j % 2))
     many = len(packs)
-
-    def count(c, busy):
-        return busy + jnp.where(pairs[2, c * chunk] != 0, 1, 0)
-
-    busy = lax.fori_loop(0, chunks, count, 0)
 
     def on_units(*units):
         def push(i, rhs):
@@ -116,6 +105,17 @@
                 collect(*((before, i - LAG + many) if i < LAG else (c, i - LAG)))
             return carry
 
+        get_order.wait()
+        for p in range(books):
+            owner = p // per_owner
+            place = (owner // 2) * per_owner + p % per_owner
+            position[order[p]] = place + half * ((owner & 1) ^ core)
+        get_pairs.wait()
+
+        def count(c, busy):
+            return busy + jnp.where(pairs[2, c * chunk] != 0, 1, 0)
+
+        busy = lax.fori_loop(0, chunks, count, 0)
         lax.fori_loop(0, busy, work, 0)
         last = jnp.where(busy == 0, padding, busy - 1)
         for i in range(many - 2, many):
@@ -123,18 +123,18 @@
         for i in range(many - LAG, many):
             collect(last, i)
 
+        def drop(c, carry):
+            fetch(c).wait()
+            return carry
+
+        lax.fori_loop(busy, chunks, drop, 0)
+
     spot = []
     held = []
     for _, size, unit, _ in packs:
         spot.append(len(held))
         held += [pltpu.ACC(unit)((rows, 2 * block), jnp.float32)] * (4 if size == 4 else 1)
     pl.run_scoped(on_units, *held)
-
-    def drop(c, carry):
-        fetch(c).wait()
-        return carry
-
-    lax.fori_loop(busy, chunks, drop, 0)
     kept[...] = acc[:half]
     sent[...] = acc[half:books].astype(sent.dtype)
 

time: 37.4 us -> 37.8 us (1.011)
  no operation moved by 1% of the time
where the time goes in v4:
time: 37.8 us; the launch traced here: 37.2 us
  blocking collectives  26 us (69%)
  Pallas kernels  3.62 us (10%)
  waiting for transfers between devices  2.94 us (8%)
  other arithmetic  1.71 us (5%)
  starting transfers between devices  1.66 us (4%)
  local copies, waits for them, and re-layouts  0.68 us (2%)
  between operations  0.68 us (2%)
    all_to_all x1, blocking collectives, shards(): incoming = lax.all_to_all(outgoing, 'blk', 0, 0)  14.1 us
    all_to_all x1, blocking collectives, shards(): arrived = lax.all_to_all(chip_sum, 'blk', 0, 0, axis_index_groups=same_core)  11.9 us
    pallas_call x1, Pallas kernels, shards(): pl.pallas_call(functools.partial(accumulate, groups), in_specs=[VMEM, HBM...  3.62 us
    ppermute x1, starting transfers between devices, shards(): squares = squares + lax.ppermute(squares, 'scen', [(0, 1), (1, 0)])  1.58 us
    ppermute x1, waiting for transfers between devices, shards(): across = lax.ppermute(sent, 'blk', siblings)  1.52 us
    ppermute x1, waiting for transfers between devices, shards(): squares = squares + lax.ppermute(squares, 'scen', [(0, 1), (1, 0)])  1.41 us
    convert_element_type x1, other arithmetic, shards(): (returns.astype(jnp.float32) * vol_now[None, :] / vol_hist).astype(jnp.bf...  1 us
  transfers between devices with their start and end apart: 2, of which 2 were waited for; matrix products, arithmetic and copies ran while one was open for 2% of the time, Pallas kernels for 0%

profile of v4, /device:TPU:0, one launch (start us, length us, event | category | flops | bytes accessed | tf_op | source)
XLA Modules:
  0.0 37.2 jit_solution(4515788793295864315)
XLA Ops:
  0.6 1.0 %fusion = bf16[4,8192]{1,0:T(4,128)(2,1)S(1)} fusion(f32[4,8192]{1,0:T(4,128)} %param.7, bf16[4,8192]{1,0:T(4,128)(2,1)} %param.6, f32[8192]{0:T(1024)} %param.8), kind=kLoop, calls=%fused_computation.3 | loop fusion | flops 131072 | bytes 294912 | tf_op jit(solution)/shard_map/convert_element_type | solution.py:150
  1.6 14.1 %all_to_all.10 = bf16[16,4,512]{2,1,0:T(4,128)(2,1)S(1)} all-to-all(bf16[16,4,512]{2,1,0:T(4,128)(2,1)S(1)} %bitcast.18), channel_id=1, replica_groups=mesh['scen'=2,'blk'=16] {'blk'}, dimensions={0} | all-to-all | bytes 131072 | tf_op jit(solution)/shard_map/all_to_all | solution.py:152
  15.7 3.6 %shard_map.77 = (f32[16,64,128]{2,1,0:T(8,128)S(1)}, bf16[16,64,128]{2,1,0:T(8,128)(2,1)S(1)}) custom-call(bf16[4,64,128]{2,1,0:T(8,128)(2,1)S(1)} %bitcast.16, s32[3,256]{1,0:T(4,128)} %bitcast.19, s32[32]{0:T(128)} %order_hbm.1, bf16[256,128,128]{2,1,0:T(8,128)(2,1)} %sens_hbm.1), custom_call_target="tpu_custom_call" | custom-call | flops 536870912 | bytes 8388608 | tf_op jit(solution)/shard_map/pallas_call | solution.py:155
  19.4 0.1 collective-permute-start
  19.4 1.5 %collective-permute-done = bf16[16,64,128]{2,1,0:T(8,128)(2,1)S(1)} collective-permute-done((bf16[16,64,128]{2,1,0:T(8,128)(2,1)S(1)}, bf16[16,64,128]{2,1,0:T(8,128)(2,1)S(1)}, u32[]{:S(2)}, u32[]{:S(2)}) %collective-permute-start) | collective-permute-done | bytes 262176 | tf_op jit(solution)/shard_map/ppermute | solution.py:179
  21.0 0.1 add_convert_fusion
  21.1 11.9 %all_to_all.11 = bf16[8,2,64,128]{3,2,1,0:T(8,128)(2,1)S(1)} all-to-all(bf16[8,2,64,128]{3,2,1,0:T(8,128)(2,1)S(1)} %bitcast.17), channel_id=1, replica_groups={{0,2,4,6,8,10,12,14},{1,3,5,7,9,11,13,15},{16,18,20,22,24,26,28,30},{17..., dimensions={0} | all-to-all | bytes 524288 | tf_op jit(solution)/shard_map/all_to_all | solution.py:184
  33.0 1.6 %collective-permute-start.1 = (f32[256]{0:T(256)S(1)}, f32[256]{0:T(256)S(1)}, u32[]{:S(2)}, u32[]{:S(2)}) collective-permute-start(f32[256]{0:T(256)S(1)} %bitcast.20), channel_id=1, source_target_pairs={{0,16},{16,0},{1,17},{17,1},{2,18},{18,2},{3,19},{19,3},{4,20},{20... | collective-permute-start | bytes 3080 | tf_op jit(solution)/shard_map/ppermute | solution.py:190
  34.6 0.6 %copy_bitcast_fusion = f32[64,256]{1,0:T(8,128)} fusion(f32[2,64,128]{2,1,0:T(8,128)S(1)} %convert_reduce_fusion), kind=kLoop, calls=%fused_computation.4 | loop fusion | bytes 131072 | tf_op jit(solution)/shard_map/reshape | solution.py:186
  35.3 1.4 %collective-permute-done.1 = f32[256]{0:T(256)S(1)} collective-permute-done((f32[256]{0:T(256)S(1)}, f32[256]{0:T(256)S(1)}, u32[]{:S(2)}, u32[]{:S(2)}) %collective-permute-start.1) | collective-permute-done | bytes 1056 | tf_op jit(solution)/shard_map/ppermute | solution.py:190
  36.7 0.6 %add_sqrt_fusion = f32[256]{0:T(256)} fusion(f32[256]{0:T(256)S(1)} %collective-permute-done.1, f32[2,128]{1,0:T(2,128)S(1)} %multiply_reduce_fusion), kind=kLoop, calls=%fused_computation.7 | loop fusion | flops 768 | bytes 3072 | tf_op jit(solution)/shard_map/sqrt | solution.py:193
  (4 shorter events, 0.1 us)
Async XLA Ops:
  19.4 1.6 %collective-permute-start = (bf16[16,64,128]{2,1,0:T(8,128)(2,1)S(1)}, bf16[16,64,128]{2,1,0:T(8,128)(2,1)S(1)}, u32[]{:S(2)}, u32[]{:S(2)}) collective-permute-start(bf16[16,64,128]{2,1,0:T(8,128)(2,1)S(1)} %get-tuple-element.5), channel_id=1, source_target_pairs={{0,1},{1,0},{2,3},{3,2},{4,5},{5,4},{6,7},{7,6},{8,9},{9,8},{10,11... | collective-permute-start | bytes 786440 | tf_op jit(solution)/shard_map/ppermute | solution.py:179
  33.0 3.6 %collective-permute-start.1 = (f32[256]{0:T(256)S(1)}, f32[256]{0:T(256)S(1)}, u32[]{:S(2)}, u32[]{:S(2)}) collective-permute-start(f32[256]{0:T(256)S(1)} %bitcast.20), channel_id=1, source_target_pairs={{0,16},{16,0},{1,17},{17,1},{2,18},{18,2},{3,19},{19,3},{4,20},{20... | collective-permute-start | bytes 3080 | tf_op jit(solution)/shard_map/ppermute | solution.py:190

commit v5 on v4

--- a/solution.py
+++ b/solution.py
@@ -10,6 +10,7 @@
 UNROLL = 32
 SIZES = (4, 2, 2, 4, 2, 2)
 LAG = 6
+AHEAD = 3
 VMEM_LIMIT = 32 * 1024 * 1024
 VMEM = pl.BlockSpec(memory_space=pltpu.VMEM)
 HBM = pl.BlockSpec(memory_space=pltpu.HBM)
@@ -36,7 +37,7 @@
     get_pairs = pltpu.make_async_copy(pairs_hbm, pairs.at[:, pl.ds(0, slots)], small.at[1])
     get_order.start()
     get_pairs.start()
-    for c in range(chunks):
+    for c in range(AHEAD):
         fetch(c).start()
     acc[...] = jnp.zeros_like(acc)
     position[books] = books
@@ -98,6 +99,11 @@
 
         def work(c, carry):
             fetch(c).wait()
+
+            @pl.when(c + AHEAD < busy)
+            def _():
+                fetch(c + AHEAD).start()
+
             before = jnp.where(c == 0, padding, c - 1)
             for i in range(many):
                 stage(c, i)
@@ -127,7 +133,7 @@
             fetch(c).wait()
             return carry
 
-        lax.fori_loop(busy, chunks, drop, 0)
+        lax.fori_loop(busy, AHEAD, drop, 0)
 
     spot = []
     held = []

time: 37.8 us -> 37.7 us (level); the launches traced: 37.2 us -> 37.6 us
  blocking collectives: 26 us -> 27.3 us
  Pallas kernels: 3.62 us -> 2.65 us
    all_to_all x1, blocking collectives: 11.9 us -> 13.3 us  [shards(): arrived = lax.all_to_all(chip_sum, 'blk', 0, 0, axis_index_groups=same_core)]
    pallas_call x1, Pallas kernels: 3.62 us -> 2.65 us  [shards(): pl.pallas_call(functools.partial(accumulate, groups), in_specs=[VMEM, HBM...]
where the time goes in v5:
time: 37.7 us; the launch traced here: 37.6 us
  blocking collectives  27.3 us (72%)
  waiting for transfers between devices  2.71 us (7%)
  Pallas kernels  2.65 us (7%)
  starting transfers between devices  1.89 us (5%)
  other arithmetic  1.71 us (5%)
  local copies, waits for them, and re-layouts  0.68 us (2%)
  between operations  0.67 us (2%)
    all_to_all x1, blocking collectives, shards(): incoming = lax.all_to_all(outgoing, 'blk', 0, 0)  14.1 us
    all_to_all x1, blocking collectives, shards(): arrived = lax.all_to_all(chip_sum, 'blk', 0, 0, axis_index_groups=same_core)  13.3 us
    pallas_call x1, Pallas kernels, shards(): pl.pallas_call(functools.partial(accumulate, groups), in_specs=[VMEM, HBM...  2.65 us
    ppermute x1, starting transfers between devices, shards(): squares = squares + lax.ppermute(squares, 'scen', [(0, 1), (1, 0)])  1.58 us
    ppermute x1, waiting for transfers between devices, shards(): squares = squares + lax.ppermute(squares, 'scen', [(0, 1), (1, 0)])  1.42 us
    ppermute x1, waiting for transfers between devices, shards(): across = lax.ppermute(sent, 'blk', siblings)  1.29 us
    convert_element_type x1, other arithmetic, shards(): (returns.astype(jnp.float32) * vol_now[None, :] / vol_hist).astype(jnp.bf...  1 us
  transfers between devices with their start and end apart: 2, of which 2 were waited for; matrix products, arithmetic and copies ran while one was open for 2% of the time, Pallas kernels for 0%

profile of v5, /device:TPU:0, one launch (start us, length us, event | category | flops | bytes accessed | tf_op | source)
XLA Modules:
  0.0 37.6 jit_solution(1024783078776190821)
XLA Ops:
  0.6 1.0 %fusion = bf16[4,8192]{1,0:T(4,128)(2,1)S(1)} fusion(f32[4,8192]{1,0:T(4,128)} %param.7, bf16[4,8192]{1,0:T(4,128)(2,1)} %param.6, f32[8192]{0:T(1024)} %param.8), kind=kLoop, calls=%fused_computation.3 | loop fusion | flops 131072 | bytes 294912 | tf_op jit(solution)/shard_map/convert_element_type | solution.py:156
  1.6 14.1 %all_to_all.10 = bf16[16,4,512]{2,1,0:T(4,128)(2,1)S(1)} all-to-all(bf16[16,4,512]{2,1,0:T(4,128)(2,1)S(1)} %bitcast.18), channel_id=1, replica_groups=mesh['scen'=2,'blk'=16] {'blk'}, dimensions={0} | all-to-all | bytes 131072 | tf_op jit(solution)/shard_map/all_to_all | solution.py:158
  15.7 2.7 %shard_map.77 = (f32[16,64,128]{2,1,0:T(8,128)S(1)}, bf16[16,64,128]{2,1,0:T(8,128)(2,1)S(1)}) custom-call(bf16[4,64,128]{2,1,0:T(8,128)(2,1)S(1)} %bitcast.16, s32[3,256]{1,0:T(4,128)} %bitcast.19, s32[32]{0:T(128)} %order_hbm.1, bf16[256,128,128]{2,1,0:T(8,128)(2,1)} %sens_hbm.1), custom_call_target="tpu_custom_call" | custom-call | flops 536870912 | bytes 8388608 | tf_op jit(solution)/shard_map/pallas_call | solution.py:161
  18.4 0.3 collective-permute-start
  18.7 1.3 %collective-permute-done = bf16[16,64,128]{2,1,0:T(8,128)(2,1)S(1)} collective-permute-done((bf16[16,64,128]{2,1,0:T(8,128)(2,1)S(1)}, bf16[16,64,128]{2,1,0:T(8,128)(2,1)S(1)}, u32[]{:S(2)}, u32[]{:S(2)}) %collective-permute-start) | collective-permute-done | bytes 262176 | tf_op jit(solution)/shard_map/ppermute | solution.py:185
  20.0 0.1 add_convert_fusion
  20.1 13.3 %all_to_all.11 = bf16[8,2,64,128]{3,2,1,0:T(8,128)(2,1)S(1)} all-to-all(bf16[8,2,64,128]{3,2,1,0:T(8,128)(2,1)S(1)} %bitcast.17), channel_id=1, replica_groups={{0,2,4,6,8,10,12,14},{1,3,5,7,9,11,13,15},{16,18,20,22,24,26,28,30},{17..., dimensions={0} | all-to-all | bytes 524288 | tf_op jit(solution)/shard_map/all_to_all | solution.py:190
  33.4 1.6 %collective-permute-start.1 = (f32[256]{0:T(256)S(1)}, f32[256]{0:T(256)S(1)}, u32[]{:S(2)}, u32[]{:S(2)}) collective-permute-start(f32[256]{0:T(256)S(1)} %bitcast.20), channel_id=1, source_target_pairs={{0,16},{16,0},{1,17},{17,1},{2,18},{18,2},{3,19},{19,3},{4,20},{20... | collective-permute-start | bytes 3080 | tf_op jit(solution)/shard_map/ppermute | solution.py:196
  35.0 0.6 %copy_bitcast_fusion = f32[64,256]{1,0:T(8,128)} fusion(f32[2,64,128]{2,1,0:T(8,128)S(1)} %convert_reduce_fusion), kind=kLoop, calls=%fused_computation.4 | loop fusion | bytes 131072 | tf_op jit(solution)/shard_map/reshape | solution.py:192
  35.6 1.4 %collective-permute-done.1 = f32[256]{0:T(256)S(1)} collective-permute-done((f32[256]{0:T(256)S(1)}, f32[256]{0:T(256)S(1)}, u32[]{:S(2)}, u32[]{:S(2)}) %collective-permute-start.1) | collective-permute-done | bytes 1056 | tf_op jit(solution)/shard_map/ppermute | solution.py:196
  37.0 0.6 %add_sqrt_fusion = f32[256]{0:T(256)} fusion(f32[256]{0:T(256)S(1)} %collective-permute-done.1, f32[2,128]{1,0:T(2,128)S(1)} %multiply_reduce_fusion), kind=kLoop, calls=%fused_computation.7 | loop fusion | flops 768 | bytes 3072 | tf_op jit(solution)/shard_map/sqrt | solution.py:199
  (4 shorter events, 0.1 us)
Async XLA Ops:
  18.4 1.6 %collective-permute-start = (bf16[16,64,128]{2,1,0:T(8,128)(2,1)S(1)}, bf16[16,64,128]{2,1,0:T(8,128)(2,1)S(1)}, u32[]{:S(2)}, u32[]{:S(2)}) collective-permute-start(bf16[16,64,128]{2,1,0:T(8,128)(2,1)S(1)} %get-tuple-element.5), channel_id=1, source_target_pairs={{0,1},{1,0},{2,3},{3,2},{4,5},{5,4},{6,7},{7,6},{8,9},{9,8},{10,11... | collective-permute-start | bytes 786440 | tf_op jit(solution)/shard_map/ppermute | solution.py:185
  33.4 3.6 %collective-permute-start.1 = (f32[256]{0:T(256)S(1)}, f32[256]{0:T(256)S(1)}, u32[]{:S(2)}, u32[]{:S(2)}) collective-permute-start(f32[256]{0:T(256)S(1)} %bitcast.20), channel_id=1, source_target_pairs={{0,16},{16,0},{1,17},{17,1},{2,18},{18,2},{3,19},{19,3},{4,20},{20... | collective-permute-start | bytes 3080 | tf_op jit(solution)/shard_map/ppermute | solution.py:196
